TPU v7x, 256 devices: a whole 4x4x8 slice. The times are simulated.
256 devices in a mesh: dp: 8 (over x, core), expert: 32 (over y, z).
Axes of the slice: x: 4, y: 4, z: 8, core: 2. Of those that a mesh axis runs over, the one named last changes fastest.
Arguments:
- tokens: bfloat16 [512, 7168], P('expert'), may hold values from -6 to 6
- out_grad: bfloat16 [512, 7168], P('expert'), may hold values from -6 to 6
- expert_ids: int32 [512, 8], P('expert'), may hold values from 0 to 31, all different within a row; in each aligned block of 16 rows (0 to 15, 16 to 31, ...) at most 6 rows name the same one
- gate_weights: float32 [512, 8], P('expert'), may hold values from 0.05 to 0.3
- base_gate: bfloat16 [32, 7168, 2048], P('expert', None, 'dp'), may hold values from -0.0625 to 0.0625
- base_up: bfloat16 [32, 7168, 2048], P('expert', None, 'dp'), may hold values from -0.0625 to 0.0625
- base_down: bfloat16 [32, 2048, 7168], P('expert', 'dp'), may hold values from -0.125 to 0.125
- block_ids: int32 [32, 16, 2], P('expert', 'dp'), may hold values from 0 to 167, as said below
- delta: float32 [32, 16, 2, 128, 128], P('expert', 'dp'), may hold values from -4 to 4
- moment_one: float32 [32, 16, 2, 128, 128], P('expert', 'dp'), may hold values from -0.24 to 0.24
- moment_two: float32 [32, 16, 2, 128, 128], P('expert', 'dp'), may hold values from 0.0005 to 0.005
Outputs:
- in_grad: bfloat16 [512, 7168], P('expert', 'dp')
- new_delta: float32 [32, 16, 2, 128, 128], P('expert', 'dp')
Inputs may be any that keep to these rules, and one draw needn't show every extreme that they name: `expert_ids`: each token names 8 different experts, and among the 16 tokens of one index of expert no expert is named more than 6 times. `block_ids`: the 2 ids of one column of blocks of one expert are different.
All inputs are finite; a program needn't handle non-finite values.
Results may differ from a plain program's by a relative error of at most 0.019.
Values may be sent and summed in bfloat16 or wider, within the bound.
A program may use at most 128 MiB of HBM per device.

v0:
```python
import jax
import jax.numpy as jnp
from jax import lax
from jax.sharding import PartitionSpec as P

FF = 2048
EXPERTS = 32
BLK = 128
NBLK = 2
CAP = 6


beta_one = 0.9
beta_two = 0.95
learn_rate = 0.5
adam_eps = 1e-08
corr_one = 1.0 - beta_one**10
corr_two = 1.0 - beta_two**10


def slot_tables(expert_ids, gate_weights, experts, capacity):
    flat_ids = expert_ids.reshape(-1)
    picked = (flat_ids[:, None] == jnp.arange(experts, dtype=jnp.int32)[None, :]).astype(jnp.int32)
    rank_of = jnp.sum((jnp.cumsum(picked, axis=0) - 1) * picked, axis=1)
    slot_ids = flat_ids * capacity + rank_of
    owners = jnp.arange(flat_ids.shape[0], dtype=jnp.int32) // expert_ids.shape[1]
    token_of_slot = jnp.full((experts * capacity,), -1, jnp.int32).at[slot_ids].set(owners)
    gate_of_slot = (
        jnp.zeros((experts * capacity,), jnp.float32).at[slot_ids].set(gate_weights.reshape(-1))
    )
    return (token_of_slot, gate_of_slot)


def dispatch(tokens, out_grad, token_of_slot, gate_of_slot):
    is_valid = token_of_slot >= 0
    safe_tok = jnp.maximum(token_of_slot, 0)
    rows_out = jnp.where(is_valid[:, None], tokens[safe_tok], jnp.zeros((), tokens.dtype))
    grads_out = (gate_of_slot[:, None] * out_grad[safe_tok].astype(jnp.float32)).astype(
        jnp.bfloat16
    )
    return (rows_out.reshape(EXPERTS, CAP, -1), grads_out.reshape(EXPERTS, CAP, -1))


def with_block(matrix, position, block_piece, flag):
    old_block = lax.dynamic_slice(matrix, position, (1, block_piece.shape[0], block_piece.shape[1]))
    new_block = (old_block.astype(jnp.float32) + block_piece[None]).astype(matrix.dtype)
    return lax.dynamic_update_slice(matrix, jnp.where(flag, new_block, old_block), position)


def on_device(
    tokens,
    out_grad,
    expert_ids,
    gate_weights,
    base_gate,
    base_up,
    base_down,
    block_ids,
    delta,
    moment_one,
    moment_two,
):
    loc_exp, dim_model, hid_dev = base_gate.shape
    hid_blocks = hid_dev // BLK
    dim_blocks = dim_model // BLK
    token_of_slot, gate_of_slot = slot_tables(expert_ids, gate_weights, EXPERTS, CAP)
    rows_out, grads_out = dispatch(tokens, out_grad, token_of_slot, gate_of_slot)
    rows_in, grads_in = (
        lax.all_to_all(rows_out, "expert", split_axis=0, concat_axis=1, tiled=True),
        lax.all_to_all(grads_out, "expert", split_axis=0, concat_axis=1, tiled=True),
    )
    block_kind = block_ids // dim_blocks
    row_block = block_ids % dim_blocks
    scales = jnp.where(block_kind == 2, FF ** (-0.5), dim_model ** (-0.5)).astype(jnp.float32)
    scaled = delta * scales[..., None, None]
    gate_eff, up_eff, down_eff = (base_gate, base_up, base_down)
    expert = 0
    for column in range(hid_blocks):
        for member in range(NBLK):
            kind_now = block_kind[expert, column, member]
            row_start = row_block[expert, column, member] * BLK
            block_piece = scaled[expert, column, member]
            expert_at = jnp.int32(expert)
            col_start = jnp.int32(column * BLK)
            gate_eff = with_block(
                gate_eff, (expert_at, row_start, col_start), block_piece, kind_now == 0
            )
            up_eff = with_block(
                up_eff, (expert_at, row_start, col_start), block_piece, kind_now == 1
            )
            down_eff = with_block(
                down_eff, (expert_at, col_start, row_start), block_piece, kind_now == 2
            )
    gate_pre = jnp.einsum("erd,edf->erf", rows_in, gate_eff, preferred_element_type=jnp.float32)
    up_pre = jnp.einsum("erd,edf->erf", rows_in, up_eff, preferred_element_type=jnp.float32)
    sigmoid_gate = jax.nn.sigmoid(gate_pre)
    swish_gate = gate_pre * sigmoid_gate
    hidden = (swish_gate * up_pre).astype(jnp.bfloat16)
    hidden_grad = jnp.einsum("erd,efd->erf", grads_in, down_eff, preferred_element_type=jnp.float32)
    gate_grad = (
        hidden_grad * up_pre * sigmoid_gate * (1.0 + gate_pre * (1.0 - sigmoid_gate))
    ).astype(jnp.bfloat16)
    up_grad = (hidden_grad * swish_gate).astype(jnp.bfloat16)
    partial_sum = jnp.einsum(
        "erf,edf->erd", gate_grad, gate_eff, preferred_element_type=jnp.float32
    )
    partial_sum = (
        partial_sum
        + jnp.einsum("erf,edf->erd", up_grad, up_eff, preferred_element_type=jnp.float32)
    ).astype(jnp.bfloat16)
    token_match = token_of_slot[None, :] == jnp.arange(tokens.shape[0], dtype=jnp.int32)[:, None]
    summed = lax.psum_scatter(partial_sum, "dp", scatter_dimension=2, tiled=True).astype(
        jnp.float32
    )
    returned = lax.all_to_all(
        summed.astype(jnp.bfloat16), "expert", split_axis=1, concat_axis=0, tiled=True
    ).astype(summed.dtype)
    in_part = jnp.dot(
        token_match.astype(jnp.float32),
        returned.reshape(EXPERTS * CAP, -1),
        precision=lax.Precision.HIGHEST,
    )
    in_grad = in_part.astype(jnp.bfloat16)
    grad_list = []
    expert = 0
    for column in range(hid_blocks):
        for member in range(NBLK):
            kind_now = block_kind[expert, column, member]
            row_start = row_block[expert, column, member] * BLK
            x_part = lax.dynamic_slice_in_dim(rows_in[expert], row_start, BLK, 1)
            y_part = lax.dynamic_slice_in_dim(grads_in[expert], row_start, BLK, 1)
            h_part = hidden[expert, :, column * BLK : (column + 1) * BLK]
            g_part = gate_grad[expert, :, column * BLK : (column + 1) * BLK]
            u_part = up_grad[expert, :, column * BLK : (column + 1) * BLK]
            left_part = jnp.where(kind_now == 2, h_part, x_part)
            right_part = jnp.where(kind_now == 0, g_part, jnp.where(kind_now == 1, u_part, y_part))
            grad_list.append(
                lax.dot_general(
                    left_part,
                    right_part,
                    (((0,), (0,)), ((), ())),
                    preferred_element_type=jnp.float32,
                )
            )
    block_grads = jnp.stack(grad_list).reshape(delta.shape) * scales[..., None, None]
    mom_one = beta_one * moment_one + (1.0 - beta_one) * block_grads
    mom_two = beta_two * moment_two + (1.0 - beta_two) * block_grads * block_grads
    new_delta = delta - learn_rate * (mom_one / corr_one) / (
        jnp.sqrt(mom_two / corr_two) + adam_eps
    )
    return (in_grad, new_delta)


def solution(mesh):
    placed = (
        P("expert", None),
        P("expert", None),
        P("expert", None),
        P("expert", None),
        P("expert", None, "dp"),
        P("expert", None, "dp"),
        P("expert", "dp", None),
        P("expert", "dp", None),
        P("expert", "dp", None, None, None),
        P("expert", "dp", None, None, None),
        P("expert", "dp", None, None, None),
    )
    return jax.shard_map(
        on_device,
        mesh=mesh,
        in_specs=placed,
        out_specs=(P("expert", "dp"), P("expert", "dp", None, None, None)),
        check_vma=False,
    )
```

profile of v0, /device:TPU:8, one launch (start us, length us, event | category | flops | bytes accessed | tf_op | source)
XLA Modules:
  0.0 330.1 jit_solution(13866589108580147082)
XLA Ops:
  7.2 4.3 %copy.54 = bf16[1,7168,256]{2,1,0:T(8,128)(2,1)} copy(bf16[1,7168,256]{2,1,0:T(8,128)(2,1)} %param.16) | data formatting | bytes 7340032
  11.4 1.9 copy.53
  13.3 1.5 copy-done.8
  14.8 1.9 copy.55
  17.5 1.0 scatter_custom_fusion
  18.5 2.3 gather_fusion
  20.8 3.5 %reshape.208 = f32[32,6,7168]{2,1,0:T(8,128)} reshape(bf16[192,7168]{1,0:T(8,128)(2,1)S(1)} %gather_fusion) | data formatting | bytes 8257536 | tf_op jit(solution)/shard_map/convert_element_type | solution.py:38
  24.5 1.0 scatter_custom_fusion.1
  25.6 5.7 %multiply_convert_fusion = bf16[32,6,7168]{2,1,0:T(8,128)(2,1)} fusion(f32[32,6,7168]{2,1,0:T(8,128)} %reshape.208, f32[32,6]{1,0:T(8,128)S(1)} %mul.175), kind=kLoop, calls=%fused_computation.7 | loop fusion | flops 2752512 | bytes 8258304 | tf_op jit(solution)/shard_map/convert_element_type | solution.py:38
  31.3 11.9 %all-to-all-start = ((bf16[32,6,7168]{2,1,0:T(8,128)(2,1)}), bf16[32,6,7168]{2,1,0:T(8,128)(2,1)}, u32[]{:S(2)}, u32[]{:S(2)}) async-start(bf16[32,6,7168]{2,1,0:T(8,128)(2,1)} %multiply_convert_fusion), calls=%async_computation | async-start | bytes 7340032 | tf_op jit(solution)/shard_map/all_to_all | solution.py:70
  43.2 2.3 gather_fusion.1
  45.5 2.7 gather.10
  48.4 4.2 %broadcast_select_fusion = bf16[32,6,7168]{2,1,0:T(8,128)(2,1)} fusion(bf16[32,6,7168]{2,1,0:T(8,128)(2,1)} %gather.10, pred[32,6]{1,0:T(8,128)(4,1)S(1)} %broadcast_in_dim.46), kind=kLoop, calls=%fused_computation.9 | loop fusion | flops 1376256 | bytes 5505216 | tf_op jit(solution)/shard_map/jit(_where)/select_n | solution.py:37
  52.6 73.1 %all-to-all-done = bf16[32,6,7168]{2,1,0:T(8,128)(2,1)} async-done(((bf16[32,6,7168]{2,1,0:T(8,128)(2,1)}), bf16[32,6,7168]{2,1,0:T(8,128)(2,1)}, u32[]{:S(2)}, u32[]{:S(2)}) %all-to-all-start) | async-done | bytes 2752544 | tf_op jit(solution)/shard_map/all_to_all | solution.py:70
  125.7 8.2 %all-to-all-start.1 = ((bf16[32,6,7168]{2,1,0:T(8,128)(2,1)}), bf16[32,6,7168]{2,1,0:T(8,128)(2,1)}, u32[]{:S(2)}, u32[]{:S(2)}) async-start(bf16[32,6,7168]{2,1,0:T(8,128)(2,1)} %broadcast_select_fusion), calls=%async_computation.1 | async-start | bytes 7340032 | tf_op jit(solution)/shard_map/all_to_all | solution.py:69
  146.1 1.4 fusion.66
  147.5 1.5 fusion.65
  149.0 1.5 fusion.64
  150.4 1.4 fusion.69
  151.9 4.3 %copy.48 = bf16[7168,256]{1,0:T(8,128)(2,1)} copy(bf16[7168,256]{1,0:T(8,128)(2,1)} %bitcast.210) | data formatting | bytes 7340032
  156.2 1.9 copy.49
  158.0 1.5 copy-done.5
  159.5 1.8 copy.47
  161.4 1.5 fusion.63
  162.8 3.2 reshape.198
  166.1 4.4 %fusion.85 = f32[192,256]{1,0:T(8,128)S(1)} fusion(bf16[192,7168]{1,0:T(8,128)(2,1)S(1)} %reshape.198, bf16[256,7168]{1,0:T(8,128)(2,1)} %get-tuple-element.9), kind=kOutput, calls=%fused_computation.145 | convolution fusion | flops 704643072 | bytes 6619136 | tf_op jit(solution)/shard_map/erd,efd->erf/dot_general | solution.py:99
  170.5 46.4 %all-to-all-done.1 = bf16[32,6,7168]{2,1,0:T(8,128)(2,1)} async-done(((bf16[32,6,7168]{2,1,0:T(8,128)(2,1)}), bf16[32,6,7168]{2,1,0:T(8,128)(2,1)}, u32[]{:S(2)}, u32[]{:S(2)}) %all-to-all-start.1) | async-done | bytes 2752544 | tf_op jit(solution)/shard_map/all_to_all | solution.py:69
  216.9 3.2 reshape.201
  220.1 3.1 fusion.86
  223.2 0.9 fusion.11
  224.2 1.4 fusion.87
  226.3 3.0 fusion.1
  229.2 16.1 %copy.27 = bf16[1,192,7168]{1,0,2:T(2,128)(2,1)} copy(bf16[1,192,7168]{2,1,0:T(8,128)(2,1)} %fusion.1) | data formatting | bytes 5505024
  245.3 5.6 %copy.37 = bf16[7168,1,192]{2,0,1:T(8,128)(2,1)} copy(bf16[7168,1,192]{2,1,0:T(2,128)(2,1)} %bitcast.209) | data formatting | bytes 5505024
  251.0 1.6 convolution_bitcast_fusion.3
  252.6 37.2 %reduce-scatter.4.cloned.1.call-done = bf16[896,192]{1,0:T(8,128)(2,1)} async-done(((bf16[7168,192]{1,0:T(8,128)(2,1)}), bf16[896,192]{1,0:T(8,128)(2,1)}) %reduce-scatter.4.cloned.1.call-update) | async-done | bytes 344080
  289.8 2.4 reshape_bitcast_fusion
  292.2 4.7 %copy.26 = bf16[1,192,896]{2,0,1:T(2,128)(2,1)} copy(bf16[1,192,896]{1,0,2:T(2,128)(2,1)} %reshape_bitcast_fusion) | data formatting | bytes 688128 | tf_op jit(solution)/shard_map/reduce_scatter | solution.py:112
  297.4 3.6 %reduce = bf16[192,896]{1,0:T(8,128)(2,1)S(1)} reduce(bf16[192,1,896]{2,1,0:T(2,128)(2,1)} %bitcast.214, bf16[]{:T(256)} %broadcast.141), dimensions={1}, to_apply=%bitcast.196.reduce_sub_computation | reduce | bytes 688130
  301.1 0.9 reshape.250
  302.0 10.0 %all-to-all-start.2 = ((bf16[32,2,2688]{2,1,0:T(2,128)(2,1)}), bf16[32,2,2688]{2,1,0:T(2,128)(2,1)S(1)}, u32[]{:S(2)}, u32[]{:S(2)}) async-start(bf16[32,2,2688]{2,1,0:T(2,128)(2,1)} %reshape.250), calls=%async_computation.2 | async-start | bytes 688128 | tf_op jit(solution)/shard_map/all_to_all | solution.py:115
  312.0 1.0 convolution_bitcast_fusion.2
  313.0 1.0 convolution_bitcast_fusion.1
  314.1 1.0 convolution_bitcast_fusion
  315.1 0.9 pad_maximum_fusion
  316.0 2.1 fusion.9
  318.1 4.1 %all-to-all-done.2 = bf16[32,2,2688]{2,1,0:T(2,128)(2,1)S(1)} async-done(((bf16[32,2,2688]{2,1,0:T(2,128)(2,1)}), bf16[32,2,2688]{2,1,0:T(2,128)(2,1)S(1)}, u32[]{:S(2)}, u32[]{:S(2)}) %all-to-all-start.2) | async-done | bytes 344096 | tf_op jit(solution)/shard_map/all_to_all | solution.py:115
  322.5 0.8 convolution_convert_fusion
  (54 shorter events, 4.4 us)
Async XLA Ops:
  7.2 11.4 %copy-start = (bf16[16,7168]{1,0:T(8,128)(2,1)S(1)}, bf16[16,7168]{1,0:T(8,128)(2,1)}, u32[]{:S(2)}) copy-start(bf16[16,7168]{1,0:T(8,128)(2,1)} %param.12) | copy-start | bytes 688132
  7.2 4.3 %copy-start.7 = (bf16[1,7168,256]{2,1,0:T(8,128)(2,1)S(1)}, bf16[1,7168,256]{2,1,0:T(8,128)(2,1)}, u32[]{:S(2)}) copy-start(bf16[1,7168,256]{2,1,0:T(8,128)(2,1)} %param.15) | copy-start | bytes 11010052
  11.4 3.4 %copy-start.8 = (bf16[1,256,7168]{2,1,0:T(8,128)(2,1)S(1)}, bf16[1,256,7168]{2,1,0:T(8,128)(2,1)}, u32[]{:S(2)}) copy-start(bf16[1,256,7168]{2,1,0:T(8,128)(2,1)} %param.17) | copy-start | bytes 11010052
  14.8 1.9 copy-start.11
  20.8 3.5 %copy-start.12 = (f32[16,8]{0,1:T(8,128)S(1)}, f32[16,8]{0,1:T(8,128)}, u32[]{:S(2)}) copy-start(f32[16,8]{0,1:T(8,128)} %param.14) | copy-start | bytes 1540
  31.3 11.9 %copy-start.2 = (bf16[16,7168]{1,0:T(8,128)(2,1)S(1)}, bf16[16,7168]{1,0:T(8,128)(2,1)}, u32[]{:S(2)}) copy-start(bf16[16,7168]{1,0:T(8,128)(2,1)} %param.11) | copy-start | bytes 688132
  31.3 94.4 %all-to-all-start = ((bf16[32,6,7168]{2,1,0:T(8,128)(2,1)}), bf16[32,6,7168]{2,1,0:T(8,128)(2,1)}, u32[]{:S(2)}, u32[]{:S(2)}) async-start(bf16[32,6,7168]{2,1,0:T(8,128)(2,1)} %multiply_convert_fusion), calls=%async_computation | async-start | bytes 7340032 | tf_op jit(solution)/shard_map/all_to_all | solution.py:70
  52.6 81.6 %copy-start.13 = (s32[1,2,2]{2,1,0:T(2,128)S(1)}, s32[1,2,2]{2,1,0:T(2,128)}, u32[]{:S(2)}) copy-start(s32[1,2,2]{2,1,0:T(2,128)} %param.18) | copy-start | bytes 52
  52.6 93.4 %copy-start.10 = (f32[1,2,2,128,128]{4,3,2,1,0:T(8,128)S(1)}, f32[1,2,2,128,128]{4,3,2,1,0:T(8,128)}, u32[]{:S(2)}) copy-start(f32[1,2,2,128,128]{4,3,2,1,0:T(8,128)} %param.19) | copy-start | bytes 786436
  125.7 91.1 %all-to-all-start.1 = ((bf16[32,6,7168]{2,1,0:T(8,128)(2,1)}), bf16[32,6,7168]{2,1,0:T(8,128)(2,1)}, u32[]{:S(2)}, u32[]{:S(2)}) async-start(bf16[32,6,7168]{2,1,0:T(8,128)(2,1)} %broadcast_select_fusion), calls=%async_computation.1 | async-start | bytes 7340032 | tf_op jit(solution)/shard_map/all_to_all | solution.py:69
  134.0 155.8 %reduce-scatter.4.cloned.1.call-start = ((), (), s32[]{:S(2)}) async-start(), calls=%async_computation.4 | async-start | bytes 4128768
  151.9 4.3 %copy-start.4 = (bf16[1,256,7168]{2,1,0:T(8,128)(2,1)S(1)}, bf16[1,256,7168]{2,1,0:T(8,128)(2,1)}, u32[]{:S(2)}) copy-start(bf16[1,256,7168]{2,1,0:T(8,128)(2,1)} %get-tuple-element.16) | copy-start | bytes 11010052
  156.2 3.4 %copy-start.5 = (bf16[1,7168,256]{2,1,0:T(8,128)(2,1)S(1)}, bf16[1,7168,256]{2,1,0:T(8,128)(2,1)}, u32[]{:S(2)}) copy-start(bf16[1,7168,256]{2,1,0:T(8,128)(2,1)} %get-tuple-element.10) | copy-start | bytes 11010052
  166.1 4.4 %copy-start.9 = (bf16[192,7168]{1,0:T(8,128)(2,1)}, bf16[192,7168]{1,0:T(8,128)(2,1)S(1)}, u32[]{:S(2)}) copy-start(bf16[192,7168]{1,0:T(8,128)(2,1)S(1)} %reshape.198) | copy-start | bytes 8257540
  220.1 3.1 copy-start.6
  224.2 26.8 %copy-start.14 = (bf16[1,192,256]{2,1,0:T(8,128)(2,1)}, bf16[1,192,256]{2,1,0:T(8,128)(2,1)S(1)}, u32[]{:S(2)}) copy-start(bf16[1,192,256]{2,1,0:T(8,128)(2,1)S(1)} %get-tuple-element.4) | copy-start | bytes 294916
  224.2 2.1 copy-start.3
  292.2 31.1 %copy-start.1 = (bf16[16,7168]{1,0:T(8,128)(2,1)S(1)}, bf16[16,7168]{1,0:T(8,128)(2,1)}, u32[]{:S(2)}) copy-start(bf16[16,7168]{1,0:T(8,128)(2,1)} %param.12) | copy-start | bytes 688132
  302.0 20.2 %all-to-all-start.2 = ((bf16[32,2,2688]{2,1,0:T(2,128)(2,1)}), bf16[32,2,2688]{2,1,0:T(2,128)(2,1)S(1)}, u32[]{:S(2)}, u32[]{:S(2)}) async-start(bf16[32,2,2688]{2,1,0:T(2,128)(2,1)} %reshape.250), calls=%async_computation.2 | async-start | bytes 688128 | tf_op jit(solution)/shard_map/all_to_all | solution.py:115
Sparse Core Ops, SparseCore 0:
  251.1 38.6 reduce-scatter.3
where the time goes:
time: 334 us; the launch traced here: 330 us
  waiting for transfers between devices  161 us (48%)
  local copies, waits for them, and re-layouts  71.6 us (21%)
  starting transfers between devices  30.4 us (9%)
  between operations  24.8 us (7%)
  other arithmetic  24.3 us (7%)
  matrix products  18.2 us (5%)
    all_to_all x1, waiting for transfers between devices, on_device(): lax.all_to_all(grads_out, 'expert', split_axis=0, concat_axis=1, tiled=True)  73.1 us
    all_to_all x1, waiting for transfers between devices, on_device(): lax.all_to_all(rows_out, 'expert', split_axis=0, concat_axis=1, tiled=True)  46.4 us
    unnamed x44, local copies, waits for them, and re-layouts  45.8 us
    unnamed x2, waiting for transfers between devices  37.2 us
    all_to_all x1, starting transfers between devices, on_device(): lax.all_to_all(grads_out, 'expert', split_axis=0, concat_axis=1, tiled=True)  11.9 us
    all_to_all x1, starting transfers between devices, on_device(): lax.all_to_all(summed.astype(jnp.bfloat16), 'expert', split_axis=1, conca...  10 us
    all_to_all x1, starting transfers between devices, on_device(): lax.all_to_all(rows_out, 'expert', split_axis=0, concat_axis=1, tiled=True)  8.25 us
    dynamic_update_slice x5, other arithmetic, with_block(): lax.dynamic_update_slice(matrix, jnp.where(flag, new_block, old_block), p...  7.22 us
  transfers between devices with their start and end apart: 4, of which 4 were waited for; matrix products, arithmetic and copies ran while one was open for 12% of the time, Pallas kernels for 0%

commit v1 on v0

v1 whole, which is shorter than its diff:
```python
import functools

import jax
import jax.numpy as jnp
from jax import lax
from jax.experimental import pallas as pl
from jax.experimental.pallas import tpu as pltpu
from jax.sharding import PartitionSpec as P

D = 7168
FF = 2048
BLK = 128
CAP = 6
PAD = 8
TOK = 16
TOP = 8
HID = 256
ROWS = 192
HALF = ROWS // 2
FEAT = 896
FBLK = D // BLK
NT_DEV = FEAT // BLK
CHUNKS = ((0, 512), (512, 384))
NCH = len(CHUNKS)
WIDE = 256

beta_one = 0.9
beta_two = 0.95
learn_rate = 0.5
adam_eps = 1e-08
corr_one = 1.0 - beta_one**10
corr_two = 1.0 - beta_two**10

MESH = pl.DeviceIdType.MESH
F32 = jnp.float32
BF16 = jnp.bfloat16
NT = (((1,), (1,)), ((), ()))
TN = (((0,), (0,)), ((), ()))


def mm(a, b):
    return jnp.dot(a, b, preferred_element_type=F32)


def mm_nt(a, b):
    return lax.dot_general(a, b, NT, preferred_element_type=F32)


def mm_tn(a, b):
    return lax.dot_general(a, b, TN, preferred_element_type=F32)


def slot_matrix(ids_t, gates_t, count, width_bits):
    place = lax.broadcasted_iota(jnp.int32, (count, TOK), 0)
    expert = place >> width_bits
    rank = (place & (PAD - 1)).astype(F32)
    named = jnp.zeros((count, TOK), F32)
    gates = jnp.zeros((count, TOK), F32)
    for k in range(TOP):
        hit = expert == ids_t[k : k + 1, :]
        named = jnp.where(hit, 1.0, named)
        gates = jnp.where(hit, gates_t[k : k + 1, :], gates)
    earlier = (
        lax.broadcasted_iota(jnp.int32, (TOK, TOK), 0)
        < lax.broadcasted_iota(jnp.int32, (TOK, TOK), 1)
    ).astype(F32)
    before = mm(named.astype(BF16), earlier.astype(BF16))
    chosen = jnp.where(before == rank, named, 0.0)
    return chosen, gates


def kernel(
    nexp,
    ndp,
    ids_ref,
    gates_ref,
    bids,
    tok_hbm,
    og_hbm,
    wg_hbm,
    wu_hbm,
    wd_hbm,
    delta_hbm,
    m1_hbm,
    m2_hbm,
    in_grad,
    new_delta,
    tok_v,
    og_v,
    msg,
    recv,
    gath,
    wgu,
    wd,
    delta_v,
    m1_v,
    m2_v,
    dz,
    gu_acc,
    hg_acc,
    gu_b,
    hid_b,
    p_send,
    p_recv,
    far_s,
    right_s,
    left_s,
    right_t,
    left_t,
    own_t,
    far_l,
    far_r,
    from_l,
    from_r,
    msg_d,
    recv_d,
    load_sem,
    a_send,
    a_recv,
    a_loc,
    g_send,
    g_recv,
    p_ssem,
    p_rsem,
    x_ssem,
    x_rsem,
    d_send,
    d_recv,
    d_loc,
):
    me_d = lax.axis_index("dp")
    me_e = lax.axis_index("expert")
    core = lax.rem(me_d, 2)
    flip = 1 - 2 * core
    partner = me_d + flip
    right = lax.rem(me_d + 2, ndp)
    left = lax.rem(me_d + ndp - 2, ndp)
    far = lax.rem(me_d + 4, ndp)

    barrier = pltpu.get_barrier_semaphore()

    def greet(i, carry):
        pl.semaphore_signal(
            barrier, inc=1, device_id={"expert": lax.rem(me_e + i, nexp)}, device_id_type=MESH
        )
        return carry

    lax.fori_loop(1, nexp, greet, 0)
    for other in (partner, right, left):
        pl.semaphore_signal(barrier, inc=1, device_id={"dp": other}, device_id_type=MESH)

    first = pl.multiple_of(me_d * FEAT, BLK)
    loads = [
        pltpu.make_async_copy(tok_hbm.at[:, pl.ds(first, FEAT)], tok_v, load_sem.at[0]),
        pltpu.make_async_copy(og_hbm.at[:, pl.ds(first, FEAT)], og_v, load_sem.at[1]),
        pltpu.make_async_copy(delta_hbm.at[0], delta_v, load_sem.at[2]),
        pltpu.make_async_copy(wg_hbm.at[0], wgu.at[:, pl.ds(0, HID)], load_sem.at[3]),
        pltpu.make_async_copy(wu_hbm.at[0], wgu.at[:, pl.ds(HID, HID)], load_sem.at[4]),
        pltpu.make_async_copy(wd_hbm.at[0], wd, load_sem.at[5]),
        pltpu.make_async_copy(m1_hbm.at[0], m1_v, load_sem.at[6]),
        pltpu.make_async_copy(m2_hbm.at[0], m2_v, load_sem.at[7]),
    ]
    for load in loads:
        load.start()

    ids_t = ids_ref[...]
    gates_t = gates_ref[...]
    chosen, gates = slot_matrix(ids_t, gates_t, nexp * PAD, 3)
    gate_of = jnp.sum(chosen * gates, axis=1, keepdims=True)
    chosen_b = chosen.astype(BF16)
    loads[0].wait()
    loads[1].wait()
    for off, width in CHUNKS:
        cols = pl.ds(off, width)
        rows_out = mm(chosen_b, tok_v[:, cols])
        grads_out = mm(chosen_b, og_v[:, cols]) * gate_of
        msg[:, :, cols] = jnp.concatenate(
            [rows_out.reshape(nexp, PAD, width), grads_out.reshape(nexp, PAD, width)], axis=1
        ).astype(BF16)

    pl.semaphore_wait(barrier, nexp - 1 + 3)

    a_own = []
    for c, (off, width) in enumerate(CHUNKS):
        cols = pl.ds(off, width)

        def send(i, carry, c=c, cols=cols):
            to = lax.rem(me_e + i, nexp)
            pltpu.make_async_remote_copy(
                src_ref=msg.at[to, :, cols],
                dst_ref=recv.at[me_e, :, cols],
                send_sem=a_send.at[c],
                recv_sem=a_recv.at[c],
                device_id={"expert": to},
                device_id_type=MESH,
            ).start()
            return carry

        lax.fori_loop(1, nexp, send, 0)
        own = pltpu.make_async_copy(msg.at[me_e, :, cols], recv.at[me_e, :, cols], a_loc.at[c])
        own.start()
        a_own.append(own)

    loads[2].wait()
    for c in range(2):
        for m in range(2):
            scale = jnp.where(bids[0, c, m] >= 2 * FBLK, FF**-0.5, D**-0.5).astype(F32)
            dz[3 * c + m] = delta_v[c, m] * scale
        dz[3 * c + 2] = jnp.zeros((BLK, BLK), F32)
    for i in (3, 4, 5):
        loads[i].wait()

    def which(c, want):
        return 3 * c + jnp.where(bids[0, c, 0] == want, 0, jnp.where(bids[0, c, 1] == want, 1, 2))

    def adjust(j, carry):
        at = pl.ds(pl.multiple_of(j * BLK, BLK), BLK)
        for kind in range(2):
            for c in range(2):
                lanes = pl.ds(kind * HID + c * BLK, BLK)
                old = wgu[at, lanes].astype(F32)
                wgu[at, lanes] = (old + dz[which(c, kind * FBLK + j)]).astype(BF16)
        for c in range(2):
            subl = pl.ds(c * BLK, BLK)
            old = wd[subl, at].astype(F32)
            wd[subl, at] = (old + dz[which(c, 2 * FBLK + j)]).astype(BF16)
        return carry

    lax.fori_loop(0, FBLK, adjust, 0)

    gu_acc[...] = jnp.zeros_like(gu_acc)
    hg_acc[...] = jnp.zeros_like(hg_acc)

    row_i = lax.broadcasted_iota(jnp.int32, (2 * ROWS, nexp * 16), 0)
    col_i = lax.broadcasted_iota(jnp.int32, (2 * ROWS, nexp * 16), 1)
    col_r = col_i & (PAD - 1)
    want = (col_i >> 4) * CAP + col_r + jnp.where((col_i & PAD) != 0, ROWS, 0)
    compact = jnp.where((row_i == want) & (col_r < CAP), 1.0, 0.0).astype(BF16)

    def other(d):
        return d + flip

    both = pl.ds(0, 2 * ROWS)
    rows_s = pl.ds(0, ROWS)
    grads_s = pl.ds(ROWS, ROWS)

    def part(c, idx, d, which_rows, to):
        off, width = CHUNKS[c]
        ref = gath.at[pl.ds(d * NT_DEV + off // BLK, width // BLK), which_rows, :]
        return pltpu.make_async_remote_copy(
            src_ref=ref,
            dst_ref=ref,
            send_sem=g_send.at[c, idx],
            recv_sem=g_recv.at[c, idx],
            device_id={"dp": to},
            device_id_type=MESH,
        )

    sent = []

    def go(copy):
        copy.start()
        sent.append(copy)

    def held(c, d, which_rows):
        off, width = CHUNKS[c]
        at = d * NT_DEV + off // BLK
        return jnp.concatenate([gath[at + t, which_rows] for t in range(width // BLK)], axis=1)

    def use_rows(c, d):
        off, width = CHUNKS[c]
        at = pl.ds(pl.multiple_of(d * FEAT + off, BLK), width)
        gu_acc[...] += mm(held(c, d, rows_s), wgu[at, :])

    def use_grads(c, d):
        off, width = CHUNKS[c]
        at = pl.ds(pl.multiple_of(d * FEAT + off, BLK), width)
        hg_acc[...] += mm_nt(held(c, d, grads_s), wd[:, at])

    def take_own(c):
        off, width = CHUNKS[c]
        cols = pl.ds(off, width)
        a_own[c].wait()
        rest = recv.at[pl.ds(0, nexp - 1), :, cols]
        pltpu.make_async_copy(rest, rest, a_recv.at[c]).wait()
        got = recv[:, :, cols].reshape(nexp * 16, width)
        packed = mm(compact, got).astype(BF16)
        for t in range(width // BLK):
            gath[me_d * NT_DEV + off // BLK + t] = packed[:, t * BLK : (t + 1) * BLK]
        go(part(c, 0, me_d, rows_s, right))
        go(part(c, 1, me_d, grads_s, left))
        go(part(c, 2, me_d, grads_s, right))
        go(part(c, 3, me_d, rows_s, left))
        go(part(c, 6, me_d, both, partner))
        use_rows(c, me_d)
        use_grads(c, me_d)

    def take_near_first(c):
        part(c, 0, left, rows_s, me_d).wait_recv()
        go(part(c, 4, left, rows_s, right))
        go(part(c, 7, left, rows_s, partner))
        part(c, 1, right, grads_s, me_d).wait_recv()
        go(part(c, 5, right, grads_s, left))
        go(part(c, 8, right, grads_s, partner))
        use_rows(c, left)
        use_grads(c, right)
        part(c, 6, partner, both, me_d).wait_recv()
        use_rows(c, partner)
        use_grads(c, partner)

    def take_near_second(c):
        part(c, 2, left, grads_s, me_d).wait_recv()
        go(part(c, 9, left, grads_s, partner))
        part(c, 3, right, rows_s, me_d).wait_recv()
        go(part(c, 10, right, rows_s, partner))
        use_grads(c, left)
        use_rows(c, right)
        part(c, 7, other(left), rows_s, me_d).wait_recv()
        part(c, 8, other(right), grads_s, me_d).wait_recv()
        use_rows(c, other(left))
        use_grads(c, other(right))

    def take_far(c):
        part(c, 4, far, rows_s, me_d).wait_recv()
        go(part(c, 11, far, rows_s, partner))
        part(c, 5, far, grads_s, me_d).wait_recv()
        go(part(c, 12, far, grads_s, partner))
        use_rows(c, far)
        use_grads(c, far)
        part(c, 9, other(left), grads_s, me_d).wait_recv()
        part(c, 10, other(right), rows_s, me_d).wait_recv()
        use_grads(c, other(left))
        use_rows(c, other(right))

    def take_last(c):
        part(c, 11, other(far), rows_s, me_d).wait_recv()
        use_rows(c, other(far))
        part(c, 12, other(far), grads_s, me_d).wait_recv()
        use_grads(c, other(far))

    take_own(0)
    take_near_first(0)
    take_own(1)
    take_near_second(0)
    take_far(0)
    take_near_first(1)
    take_last(0)
    take_near_second(1)
    take_far(1)
    take_last(1)

    gate_pre = gu_acc[:, :HID]
    up_pre = gu_acc[:, HID:]
    hidden_grad = hg_acc[...]
    sig = jax.nn.sigmoid(gate_pre)
    swish = gate_pre * sig
    hid_b[...] = (swish * up_pre).astype(BF16)
    gu_b[:, :HID] = (hidden_grad * up_pre * sig * (1.0 + gate_pre * (1.0 - sig))).astype(BF16)
    gu_b[:, HID:] = (hidden_grad * swish).astype(BF16)

    targets = (far, right, left, me_d)

    def term(c, d):
        off, width = CHUNKS[c]
        at = pl.ds(pl.multiple_of(d * FEAT + off, BLK), width)
        return mm_nt(gu_b[...], wgu[at, :])

    def pair(c, j):
        cols = pl.ds(*CHUNKS[c])
        return pltpu.make_async_remote_copy(
            src_ref=p_send.at[j, :, cols],
            dst_ref=p_recv.at[j, :, cols],
            send_sem=p_ssem.at[c, j],
            recv_sem=p_rsem.at[c, j],
            device_id={"dp": partner},
            device_id_type=MESH,
        )

    def ring(c, idx, src, dst, to):
        return pltpu.make_async_remote_copy(
            src_ref=src,
            dst_ref=dst,
            send_sem=x_ssem.at[c, idx],
            recv_sem=x_rsem.at[c, idx],
            device_id={"dp": to},
            device_id_type=MESH,
        )

    low = pl.ds(0, HALF)
    high = pl.ds(HALF, HALF)

    def ring_copies(c):
        cols = pl.ds(*CHUNKS[c])
        return (
            ring(c, 0, far_s.at[low, cols], far_l.at[:, cols], right),
            ring(c, 1, far_s.at[high, cols], far_r.at[:, cols], left),
            ring(c, 2, right_s.at[high, cols], from_l.at[high, cols], right),
            ring(c, 3, left_s.at[low, cols], from_r.at[low, cols], left),
            ring(c, 4, right_s.at[low, cols], from_l.at[low, cols], right),
            ring(c, 5, left_s.at[high, cols], from_r.at[high, cols], left),
        )

    def give_partner(c, j):
        cols = pl.ds(*CHUNKS[c])
        p_send[j, :, cols] = term(c, other(targets[j])).astype(BF16)
        go(pair(c, j))

    def summed(c, j):
        cols = pl.ds(*CHUNKS[c])
        value = term(c, targets[j])
        pair(c, j).wait_recv()
        return value + p_recv[j, :, cols].astype(F32)

    def ring_first(c):
        cols = pl.ds(*CHUNKS[c])
        copies = ring_copies(c)
        far_s[:, cols] = summed(c, 0).astype(BF16)
        go(copies[0])
        go(copies[1])
        value = summed(c, 1)
        right_s[high, cols] = value[HALF:].astype(BF16)
        go(copies[2])
        right_t[:, cols] = value[:HALF]
        value = summed(c, 2)
        left_s[low, cols] = value[:HALF].astype(BF16)
        go(copies[3])
        left_t[:, cols] = value[HALF:]

    def ring_second(c):
        cols = pl.ds(*CHUNKS[c])
        copies = ring_copies(c)
        copies[0].wait_recv()
        right_s[low, cols] = (right_t[:, cols] + far_l[:, cols].astype(F32)).astype(BF16)
        go(copies[4])
        copies[1].wait_recv()
        left_s[high, cols] = (left_t[:, cols] + far_r[:, cols].astype(F32)).astype(BF16)
        go(copies[5])

    back_row = lax.broadcasted_iota(jnp.int32, (nexp * PAD, ROWS), 0)
    back_col = lax.broadcasted_iota(jnp.int32, (nexp * PAD, ROWS), 1)
    back_r = back_row & (PAD - 1)
    spread = jnp.where(
        (back_col == (back_row >> 3) * CAP + back_r) & (back_r < CAP), 1.0, 0.0
    ).astype(BF16)
    d_own = []

    def give_back(c):
        off, width = CHUNKS[c]
        cols = pl.ds(off, width)
        copies = ring_copies(c)
        for i in (2, 3, 4, 5):
            copies[i].wait_recv()
        total = own_t[:, cols] + from_l[:, cols].astype(F32) + from_r[:, cols].astype(F32)
        wide = mm(spread, total.astype(BF16)).reshape(nexp, PAD, width)
        second = wide[:, :, WIDE:]
        if width < 2 * WIDE:
            second = jnp.concatenate(
                [second, jnp.zeros((nexp, PAD, 2 * WIDE - width), F32)], axis=2
            )
        msg_d[c] = jnp.concatenate([wide[:, :, :WIDE], second], axis=1).astype(BF16)

        def send(i, carry):
            to = lax.rem(me_e + i, nexp)
            pltpu.make_async_remote_copy(
                src_ref=msg_d.at[c, to],
                dst_ref=recv_d.at[c, me_e],
                send_sem=d_send.at[c],
                recv_sem=d_recv.at[c],
                device_id={"expert": to},
                device_id_type=MESH,
            ).start()
            return carry

        lax.fori_loop(1, nexp, send, 0)
        own = pltpu.make_async_copy(msg_d.at[c, me_e], recv_d.at[c, me_e], d_loc.at[c])
        own.start()
        d_own.append(own)

    for j in range(4):
        give_partner(0, j)
    ring_first(0)
    for j in range(4):
        give_partner(1, j)
    ring_first(1)
    ring_second(0)
    for c in range(NCH):
        own_t[:, pl.ds(*CHUNKS[c])] = summed(c, 3)
    ring_second(1)

    loads[6].wait()
    loads[7].wait()
    for c in range(2):
        lanes = pl.ds(c * BLK, BLK)
        h_part = hid_b[:, lanes]
        g_part = gu_b[:, lanes]
        u_part = gu_b[:, pl.ds(HID + c * BLK, BLK)]
        for m in range(2):
            ident = bids[0, c, m]
            kind = jnp.where(ident >= 2 * FBLK, 2, jnp.where(ident >= FBLK, 1, 0))
            rows_both = gath[ident - kind * FBLK]
            x_part = rows_both[:ROWS]
            y_part = rows_both[ROWS:]
            lhs = jnp.where(kind == 2, h_part, x_part)
            rhs = jnp.where(kind == 0, g_part, jnp.where(kind == 1, u_part, y_part))
            scale = jnp.where(kind == 2, FF**-0.5, D**-0.5).astype(F32)
            grad = mm_tn(lhs, rhs) * scale
            mom_one = beta_one * m1_v[c, m] + (1.0 - beta_one) * grad
            mom_two = beta_two * m2_v[c, m] + (1.0 - beta_two) * grad * grad
            new_delta[0, c, m] = delta_v[c, m] - learn_rate * (mom_one / corr_one) / (
                jnp.sqrt(mom_two / corr_two) + adam_eps
            )

    chosen_d, _ = slot_matrix(ids_t, gates_t, nexp * 16, 4)
    place = lax.broadcasted_iota(jnp.int32, (nexp * 16, TOK), 0) & PAD
    upper = jnp.where(place == 0, chosen_d, 0.0).T.astype(BF16)
    lower = jnp.where(place == 0, 0.0, chosen_d).T.astype(BF16)

    for c in range(NCH):
        give_back(c)
    for c, (off, width) in enumerate(CHUNKS):
        d_own[c].wait()
        rest = recv_d.at[c, pl.ds(0, nexp - 1)]
        pltpu.make_async_copy(rest, rest, d_recv.at[c]).wait()
        got = recv_d[c].reshape(nexp * 16, WIDE)
        in_grad[:, pl.ds(off, WIDE)] = mm(upper, got).astype(BF16)
        tail = width - WIDE
        in_grad[:, pl.ds(off + WIDE, tail)] = mm(lower, got[:, :tail]).astype(BF16)

    for copy in sent:
        copy.wait_send()
    for c, (off, width) in enumerate(CHUNKS):
        rest = msg.at[pl.ds(0, nexp - 1), :, pl.ds(off, width)]
        pltpu.make_async_copy(rest, rest, a_send.at[c]).wait()
        rest = msg_d.at[c, pl.ds(0, nexp - 1)]
        pltpu.make_async_copy(rest, rest, d_send.at[c]).wait()


def on_device(
    nexp,
    ndp,
    tokens,
    out_grad,
    expert_ids,
    gate_weights,
    base_gate,
    base_up,
    base_down,
    block_ids,
    delta,
    moment_one,
    moment_two,
):
    vmem = pl.BlockSpec(memory_space=pltpu.VMEM)
    smem = pl.BlockSpec(memory_space=pltpu.SMEM)
    anym = pl.BlockSpec(memory_space=pl.ANY)
    dma = pltpu.SemaphoreType.DMA
    scratch = [
        pltpu.VMEM((TOK, FEAT), BF16),
        pltpu.VMEM((TOK, FEAT), BF16),
        pltpu.VMEM((nexp, 16, FEAT), BF16),
        pltpu.VMEM((nexp, 16, FEAT), BF16),
        pltpu.VMEM((FBLK, 2 * ROWS, BLK), BF16),
        pltpu.VMEM((D, 2 * HID), BF16),
        pltpu.VMEM((HID, D), BF16),
        pltpu.VMEM((2, 2, BLK, BLK), F32),
        pltpu.VMEM((2, 2, BLK, BLK), F32),
        pltpu.VMEM((2, 2, BLK, BLK), F32),
        pltpu.VMEM((6, BLK, BLK), F32),
        pltpu.VMEM((ROWS, 2 * HID), F32),
        pltpu.VMEM((ROWS, HID), F32),
        pltpu.VMEM((ROWS, 2 * HID), BF16),
        pltpu.VMEM((ROWS, HID), BF16),
        pltpu.VMEM((4, ROWS, FEAT), BF16),
        pltpu.VMEM((4, ROWS, FEAT), BF16),
        pltpu.VMEM((ROWS, FEAT), BF16),
        pltpu.VMEM((ROWS, FEAT), BF16),
        pltpu.VMEM((ROWS, FEAT), BF16),
        pltpu.VMEM((HALF, FEAT), F32),
        pltpu.VMEM((HALF, FEAT), F32),
        pltpu.VMEM((ROWS, FEAT), F32),
        pltpu.VMEM((HALF, FEAT), BF16),
        pltpu.VMEM((HALF, FEAT), BF16),
        pltpu.VMEM((ROWS, FEAT), BF16),
        pltpu.VMEM((ROWS, FEAT), BF16),
        pltpu.VMEM((NCH, nexp, 16, WIDE), BF16),
        pltpu.VMEM((NCH, nexp, 16, WIDE), BF16),
        dma((8,)),
        dma((NCH,)),
        dma((NCH,)),
        dma((NCH,)),
        dma((NCH, 13)),
        dma((NCH, 13)),
        dma((NCH, 4)),
        dma((NCH, 4)),
        dma((NCH, 6)),
        dma((NCH, 6)),
        dma((NCH,)),
        dma((NCH,)),
        dma((NCH,)),
    ]
    return pl.pallas_call(
        functools.partial(kernel, nexp, ndp),
        out_shape=(
            jax.ShapeDtypeStruct((TOK, FEAT), BF16),
            jax.ShapeDtypeStruct((1, 2, 2, BLK, BLK), F32),
        ),
        in_specs=[vmem, vmem, smem] + [anym] * 8,
        out_specs=(vmem, vmem),
        scratch_shapes=scratch,
        compiler_params=pltpu.CompilerParams(
            collective_id=0, has_side_effects=True, vmem_limit_bytes=56 * 1024 * 1024
        ),
    )(
        expert_ids.T,
        gate_weights.T,
        block_ids,
        tokens,
        out_grad,
        base_gate,
        base_up,
        base_down,
        delta,
        moment_one,
        moment_two,
    )


def solution(mesh):
    placed = (
        P("expert", None),
        P("expert", None),
        P("expert", None),
        P("expert", None),
        P("expert", None, "dp"),
        P("expert", None, "dp"),
        P("expert", "dp", None),
        P("expert", "dp", None),
        P("expert", "dp", None, None, None),
        P("expert", "dp", None, None, None),
        P("expert", "dp", None, None, None),
    )
    return jax.shard_map(
        functools.partial(on_device, mesh.shape["expert"], mesh.shape["dp"]),
        mesh=mesh,
        in_specs=placed,
        out_specs=(P("expert", "dp"), P("expert", "dp", None, None, None)),
        check_vma=False,
    )
```

time: 334 us -> 88 us (0.26); the launches traced: 330 us -> 87.7 us
  waiting for transfers between devices: 161 us -> 0 us
  Pallas kernels: 0 us -> 84 us
  local copies, waits for them, and re-layouts: 71.6 us -> 3.03 us
  starting transfers between devices: 30.4 us -> 0 us
  other arithmetic: 24.3 us -> 0 us
  between operations: 24.8 us -> 0.64 us
  matrix products: 18.2 us -> 0 us
    all_to_all x3 -> x0, waiting for transfers between devices: 124 us -> none  [the longest x1 73.1 us: on_device(): lax.all_to_all(grads_out, 'expert', split_axis=0, concat_axis=1, tiled=True)]
    pallas_call x0 -> x1, Pallas kernels: none -> 84 us  [on_device(): pl.pallas_call(functools.partial(kernel, nexp, ndp), out_shape=(jax.Shape...]
    unnamed x44 -> x2, local copies, waits for them, and re-layouts: 45.8 us -> 3.03 us
    unnamed x2 -> x0, waiting for transfers between devices: 37.2 us -> none
    all_to_all x3 -> x0, starting transfers between devices: 30.2 us -> none  [the longest x1 11.9 us: on_device(): lax.all_to_all(grads_out, 'expert', split_axis=0, concat_axis=1, tiled=True)]
    dot_general x10 -> x0, matrix products: 18.2 us -> none  [the longest x4 4.71 us: on_device(): lax.dot_general(left_part, right_part, (((0,), (0,)), ((), ())), preferre...]
    gather x3 -> x0, local copies, waits for them, and re-layouts: 7.31 us -> none  [the longest x2 5.02 us: dispatch(): tokens[safe_tok]]
    dynamic_update_slice x5 -> x0, other arithmetic: 7.22 us -> none  [with_block(): lax.dynamic_update_slice(matrix, jnp.where(flag, new_block, old_block), p...]
  transfers between devices with their start and end apart: 4 -> 0, of which waited for: 4 -> 0; matrix products, arithmetic and copies ran while one was open for 12% -> 0% of each run, Pallas kernels for 0% -> 0%
where the time goes in v1:
time: 88 us; the launch traced here: 87.7 us
  Pallas kernels  84 us (95%)
  local copies, waits for them, and re-layouts  3.03 us (3%)
    pallas_call x1, Pallas kernels, on_device(): pl.pallas_call(functools.partial(kernel, nexp, ndp), out_shape=(jax.Shape...  84 us
    unnamed x2, local copies, waits for them, and re-layouts  3.03 us

profile of v1, /device:TPU:8, one launch (start us, length us, event | category | flops | bytes accessed | tf_op | source)
XLA Modules:
  0.0 87.7 jit_solution(14757683612357954510)
XLA Ops:
  0.6 84.0 %shard_map.122 = (bf16[16,896]{1,0:T(8,128)(2,1)}, f32[1,2,2,128,128]{4,3,2,1,0:T(8,128)}) custom-call(s32[8,16]{1,0:T(8,128)} %bitcast.2, f32[8,16]{1,0:T(8,128)} %bitcast.3, s32[1,2,2]{2,1,0:T(2,128)} %bids.1, bf16[16,7168]{1,0:T(8,128)(2,1)} %tok_hbm.1, bf16[16,7168]{1,0:T(8,128)(2,1)} %og_hbm.1, bf16[1,7168,256]{2,1,0:T(8,128)(2,1)} %wg_hbm.1, ...), custom_call_target="tpu_custom_call" | custom-call | tf_op jit(solution)/shard_map/pallas_call | solution.py:601
  84.6 1.4 %copy.15 = bf16[16,896]{1,0:T(8,128)(2,1)} copy(bf16[16,896]{1,0:T(8,128)(2,1)} %get-tuple-element.4) | data formatting | bytes 57344
  86.0 1.7 %copy.16 = f32[1,2,2,128,128]{4,3,2,1,0:T(8,128)} copy(f32[1,2,2,128,128]{4,3,2,1,0:T(8,128)} %get-tuple-element.5) | data formatting | bytes 524288

commit v2 on v1

--- a/solution.py
+++ b/solution.py
@@ -20,9 +20,22 @@
 FEAT = 896
 FBLK = D // BLK
 NT_DEV = FEAT // BLK
-CHUNKS = ((0, 512), (512, 384))
+
+
+def cut(*widths):
+    return tuple((sum(widths[:i]), w) for i, w in enumerate(widths))
+
+
+CHUNKS = cut(128, 256, 256, 256)
 NCH = len(CHUNKS)
-WIDE = 256
+GROUPS = cut(128, 256, 256, 256)
+SUMS = cut(256, 256, 256, 128)
+NSM = len(SUMS)
+BACK = cut(256, 256, 256, 128)
+NBK = len(BACK)
+WIDE = 128
+TAKE_KEYS = (0, 0.6, 0.65, 1.1, 1.15, 1.6, 1.65, 2.1)
+GIVE_KEYS = (0, 0.5, 1.6, 2.7)
 
 beta_one = 0.9
 beta_two = 0.95
@@ -36,6 +49,16 @@
 BF16 = jnp.bfloat16
 NT = (((1,), (1,)), ((), ()))
 TN = (((0,), (0,)), ((), ()))
+
+
+def last_of(parts, whole):
+    ends = {off + width: (off, width) for off, width in whole}
+    return {c: ends[off + width] for c, (off, width) in enumerate(parts) if off + width in ends}
+
+
+def in_order(parts, keys):
+    steps = [(c + key, c, step) for c in range(parts) for step, key in enumerate(keys)]
+    return [step[1:] for step in sorted(steps)]
 
 
 def mm(a, b):
@@ -201,32 +224,40 @@
         own.start()
         a_own.append(own)
 
-    loads[2].wait()
-    for c in range(2):
-        for m in range(2):
-            scale = jnp.where(bids[0, c, m] >= 2 * FBLK, FF**-0.5, D**-0.5).astype(F32)
-            dz[3 * c + m] = delta_v[c, m] * scale
-        dz[3 * c + 2] = jnp.zeros((BLK, BLK), F32)
-    for i in (3, 4, 5):
-        loads[i].wait()
-
-    def which(c, want):
-        return 3 * c + jnp.where(bids[0, c, 0] == want, 0, jnp.where(bids[0, c, 1] == want, 1, 2))
-
-    def adjust(j, carry):
-        at = pl.ds(pl.multiple_of(j * BLK, BLK), BLK)
-        for kind in range(2):
+    def adjust_all():
+        loads[2].wait()
+        for c in range(2):
+            for m in range(2):
+                scale = jnp.where(bids[0, c, m] >= 2 * FBLK, FF**-0.5, D**-0.5).astype(F32)
+                dz[3 * c + m] = delta_v[c, m] * scale
+            dz[3 * c + 2] = jnp.zeros((BLK, BLK), F32)
+        for i in (3, 4, 5):
+            loads[i].wait()
+
+        def which(c, want):
+            return 3 * c + jnp.where(bids[0, c, 0] == want, 0, jnp.where(bids[0, c, 1] == want, 1, 2))
+
+        def adjust(j, carry):
+            at = pl.ds(pl.multiple_of(j * BLK, BLK), BLK)
+            for kind in range(2):
+                for c in range(2):
+                    lanes = pl.ds(kind * HID + c * BLK, BLK)
+                    old = wgu[at, lanes].astype(F32)
+                    wgu[at, lanes] = (old + dz[which(c, kind * FBLK + j)]).astype(BF16)
             for c in range(2):
-                lanes = pl.ds(kind * HID + c * BLK, BLK)
-                old = wgu[at, lanes].astype(F32)
-                wgu[at, lanes] = (old + dz[which(c, kind * FBLK + j)]).astype(BF16)
-        for c in range(2):
-            subl = pl.ds(c * BLK, BLK)
-            old = wd[subl, at].astype(F32)
-            wd[subl, at] = (old + dz[which(c, 2 * FBLK + j)]).astype(BF16)
-        return carry
-
-    lax.fori_loop(0, FBLK, adjust, 0)
+                subl = pl.ds(c * BLK, BLK)
+                old = wd[subl, at].astype(F32)
+                wd[subl, at] = (old + dz[which(c, 2 * FBLK + j)]).astype(BF16)
+            return carry
+
+        lax.fori_loop(0, FBLK, adjust, 0)
+
+    adjust_all()
+
+    chosen_d, _ = slot_matrix(ids_t, gates_t, nexp * 16, 4)
+    place = lax.broadcasted_iota(jnp.int32, (nexp * 16, TOK), 0) & PAD
+    upper = jnp.where(place == 0, chosen_d, 0.0).T.astype(BF16)
+    lower = jnp.where(place == 0, 0.0, chosen_d).T.astype(BF16)
 
     gu_acc[...] = jnp.zeros_like(gu_acc)
     hg_acc[...] = jnp.zeros_like(hg_acc)
@@ -262,20 +293,23 @@
         copy.start()
         sent.append(copy)
 
-    def held(c, d, which_rows):
-        off, width = CHUNKS[c]
+    def held(off, width, d, which_rows):
         at = d * NT_DEV + off // BLK
         return jnp.concatenate([gath[at + t, which_rows] for t in range(width // BLK)], axis=1)
 
+    group_of = last_of(CHUNKS, GROUPS)
+
     def use_rows(c, d):
-        off, width = CHUNKS[c]
-        at = pl.ds(pl.multiple_of(d * FEAT + off, BLK), width)
-        gu_acc[...] += mm(held(c, d, rows_s), wgu[at, :])
+        if c in group_of:
+            off, width = group_of[c]
+            at = pl.ds(pl.multiple_of(d * FEAT + off, BLK), width)
+            gu_acc[...] += mm(held(off, width, d, rows_s), wgu[at, :])
 
     def use_grads(c, d):
-        off, width = CHUNKS[c]
-        at = pl.ds(pl.multiple_of(d * FEAT + off, BLK), width)
-        hg_acc[...] += mm_nt(held(c, d, grads_s), wd[:, at])
+        if c in group_of:
+            off, width = group_of[c]
+            at = pl.ds(pl.multiple_of(d * FEAT + off, BLK), width)
+            hg_acc[...] += mm_nt(held(off, width, d, grads_s), wd[:, at])
 
     def take_own(c):
         off, width = CHUNKS[c]
@@ -304,6 +338,8 @@
         go(part(c, 8, right, grads_s, partner))
         use_rows(c, left)
         use_grads(c, right)
+
+    def take_partner(c):
         part(c, 6, partner, both, me_d).wait_recv()
         use_rows(c, partner)
         use_grads(c, partner)
@@ -315,6 +351,8 @@
         go(part(c, 10, right, rows_s, partner))
         use_grads(c, left)
         use_rows(c, right)
+
+    def take_passed_first(c):
         part(c, 7, other(left), rows_s, me_d).wait_recv()
         part(c, 8, other(right), grads_s, me_d).wait_recv()
         use_rows(c, other(left))
@@ -327,27 +365,31 @@
         go(part(c, 12, far, grads_s, partner))
         use_rows(c, far)
         use_grads(c, far)
+
+    def take_passed_second(c):
         part(c, 9, other(left), grads_s, me_d).wait_recv()
         part(c, 10, other(right), rows_s, me_d).wait_recv()
         use_grads(c, other(left))
         use_rows(c, other(right))
 
-    def take_last(c):
+    def take_passed_far(c):
         part(c, 11, other(far), rows_s, me_d).wait_recv()
         use_rows(c, other(far))
         part(c, 12, other(far), grads_s, me_d).wait_recv()
         use_grads(c, other(far))
 
-    take_own(0)
-    take_near_first(0)
-    take_own(1)
-    take_near_second(0)
-    take_far(0)
-    take_near_first(1)
-    take_last(0)
-    take_near_second(1)
-    take_far(1)
-    take_last(1)
+    takes = (
+        take_own,
+        take_near_first,
+        take_partner,
+        take_near_second,
+        take_passed_first,
+        take_far,
+        take_passed_second,
+        take_passed_far,
+    )
+    for c, step in in_order(NCH, TAKE_KEYS):
+        takes[step](c)
 
     gate_pre = gu_acc[:, :HID]
     up_pre = gu_acc[:, HID:]
@@ -361,12 +403,12 @@
     targets = (far, right, left, me_d)
 
     def term(c, d):
-        off, width = CHUNKS[c]
+        off, width = SUMS[c]
         at = pl.ds(pl.multiple_of(d * FEAT + off, BLK), width)
         return mm_nt(gu_b[...], wgu[at, :])
 
     def pair(c, j):
-        cols = pl.ds(*CHUNKS[c])
+        cols = pl.ds(*SUMS[c])
         return pltpu.make_async_remote_copy(
             src_ref=p_send.at[j, :, cols],
             dst_ref=p_recv.at[j, :, cols],
@@ -390,7 +432,7 @@
     high = pl.ds(HALF, HALF)
 
     def ring_copies(c):
-        cols = pl.ds(*CHUNKS[c])
+        cols = pl.ds(*SUMS[c])
         return (
             ring(c, 0, far_s.at[low, cols], far_l.at[:, cols], right),
             ring(c, 1, far_s.at[high, cols], far_r.at[:, cols], left),
@@ -401,18 +443,18 @@
         )
 
     def give_partner(c, j):
-        cols = pl.ds(*CHUNKS[c])
+        cols = pl.ds(*SUMS[c])
         p_send[j, :, cols] = term(c, other(targets[j])).astype(BF16)
         go(pair(c, j))
 
     def summed(c, j):
-        cols = pl.ds(*CHUNKS[c])
+        cols = pl.ds(*SUMS[c])
         value = term(c, targets[j])
         pair(c, j).wait_recv()
         return value + p_recv[j, :, cols].astype(F32)
 
     def ring_first(c):
-        cols = pl.ds(*CHUNKS[c])
+        cols = pl.ds(*SUMS[c])
         copies = ring_copies(c)
         far_s[:, cols] = summed(c, 0).astype(BF16)
         go(copies[0])
@@ -427,7 +469,7 @@
         left_t[:, cols] = value[HALF:]
 
     def ring_second(c):
-        cols = pl.ds(*CHUNKS[c])
+        cols = pl.ds(*SUMS[c])
         copies = ring_copies(c)
         copies[0].wait_recv()
         right_s[low, cols] = (right_t[:, cols] + far_l[:, cols].astype(F32)).astype(BF16)
@@ -435,6 +477,7 @@
         copies[1].wait_recv()
         left_s[high, cols] = (left_t[:, cols] + far_r[:, cols].astype(F32)).astype(BF16)
         go(copies[5])
+        own_t[:, cols] = summed(c, 3)
 
     back_row = lax.broadcasted_iota(jnp.int32, (nexp * PAD, ROWS), 0)
     back_col = lax.broadcasted_iota(jnp.int32, (nexp * PAD, ROWS), 1)
@@ -445,18 +488,15 @@
     d_own = []
 
     def give_back(c):
-        off, width = CHUNKS[c]
+        off, width = BACK[c]
         cols = pl.ds(off, width)
-        copies = ring_copies(c)
-        for i in (2, 3, 4, 5):
-            copies[i].wait_recv()
+        for p, (low_end, size) in enumerate(SUMS):
+            if off <= low_end < off + width:
+                for copy in ring_copies(p)[2:]:
+                    copy.wait_recv()
         total = own_t[:, cols] + from_l[:, cols].astype(F32) + from_r[:, cols].astype(F32)
         wide = mm(spread, total.astype(BF16)).reshape(nexp, PAD, width)
-        second = wide[:, :, WIDE:]
-        if width < 2 * WIDE:
-            second = jnp.concatenate(
-                [second, jnp.zeros((nexp, PAD, 2 * WIDE - width), F32)], axis=2
-            )
+        second = wide[:, :, WIDE:] if width > WIDE else jnp.zeros((nexp, PAD, WIDE), F32)
         msg_d[c] = jnp.concatenate([wide[:, :, :WIDE], second], axis=1).astype(BF16)
 
         def send(i, carry):
@@ -476,16 +516,19 @@
         own.start()
         d_own.append(own)
 
-    for j in range(4):
-        give_partner(0, j)
-    ring_first(0)
-    for j in range(4):
-        give_partner(1, j)
-    ring_first(1)
-    ring_second(0)
-    for c in range(NCH):
-        own_t[:, pl.ds(*CHUNKS[c])] = summed(c, 3)
-    ring_second(1)
+    def give_partner_all(c):
+        for j in range(4):
+            give_partner(c, j)
+
+    ends = last_of(SUMS, BACK)
+
+    def finish(c):
+        if c in ends:
+            give_back(BACK.index(ends[c]))
+
+    gives = (give_partner_all, ring_first, ring_second, finish)
+    for c, step in in_order(NSM, GIVE_KEYS):
+        gives[step](c)
 
     loads[6].wait()
     loads[7].wait()
@@ -510,29 +553,28 @@
                 jnp.sqrt(mom_two / corr_two) + adam_eps
             )
 
-    chosen_d, _ = slot_matrix(ids_t, gates_t, nexp * 16, 4)
-    place = lax.broadcasted_iota(jnp.int32, (nexp * 16, TOK), 0) & PAD
-    upper = jnp.where(place == 0, chosen_d, 0.0).T.astype(BF16)
-    lower = jnp.where(place == 0, 0.0, chosen_d).T.astype(BF16)
-
-    for c in range(NCH):
-        give_back(c)
-    for c, (off, width) in enumerate(CHUNKS):
+    for c, (off, width) in enumerate(BACK):
         d_own[c].wait()
         rest = recv_d.at[c, pl.ds(0, nexp - 1)]
         pltpu.make_async_copy(rest, rest, d_recv.at[c]).wait()
         got = recv_d[c].reshape(nexp * 16, WIDE)
         in_grad[:, pl.ds(off, WIDE)] = mm(upper, got).astype(BF16)
-        tail = width - WIDE
-        in_grad[:, pl.ds(off + WIDE, tail)] = mm(lower, got[:, :tail]).astype(BF16)
+        if width > WIDE:
+            in_grad[:, pl.ds(off + WIDE, WIDE)] = mm(lower, got).astype(BF16)
 
     for copy in sent:
         copy.wait_send()
     for c, (off, width) in enumerate(CHUNKS):
         rest = msg.at[pl.ds(0, nexp - 1), :, pl.ds(off, width)]
         pltpu.make_async_copy(rest, rest, a_send.at[c]).wait()
+    for c in range(NBK):
         rest = msg_d.at[c, pl.ds(0, nexp - 1)]
         pltpu.make_async_copy(rest, rest, d_send.at[c]).wait()
+
+
+def hand_on(grad_in, delta_in, grad_out, delta_out):
+    grad_out[...] = grad_in[...]
+    delta_out[...] = delta_in[...]
 
 
 def on_device(
@@ -582,23 +624,23 @@
         pltpu.VMEM((HALF, FEAT), BF16),
         pltpu.VMEM((ROWS, FEAT), BF16),
         pltpu.VMEM((ROWS, FEAT), BF16),
-        pltpu.VMEM((NCH, nexp, 16, WIDE), BF16),
-        pltpu.VMEM((NCH, nexp, 16, WIDE), BF16),
+        pltpu.VMEM((NBK, nexp, 16, WIDE), BF16),
+        pltpu.VMEM((NBK, nexp, 16, WIDE), BF16),
         dma((8,)),
         dma((NCH,)),
         dma((NCH,)),
         dma((NCH,)),
         dma((NCH, 13)),
         dma((NCH, 13)),
-        dma((NCH, 4)),
-        dma((NCH, 4)),
-        dma((NCH, 6)),
-        dma((NCH, 6)),
-        dma((NCH,)),
-        dma((NCH,)),
-        dma((NCH,)),
+        dma((NSM, 4)),
+        dma((NSM, 4)),
+        dma((NSM, 6)),
+        dma((NSM, 6)),
+        dma((NBK,)),
+        dma((NBK,)),
+        dma((NBK,)),
     ]
-    return pl.pallas_call(
+    in_grad, new_delta = pl.pallas_call(
         functools.partial(kernel, nexp, ndp),
         out_shape=(
             jax.ShapeDtypeStruct((TOK, FEAT), BF16),
@@ -623,6 +665,15 @@
         moment_one,
         moment_two,
     )
+    return pl.pallas_call(
+        hand_on,
+        out_shape=(
+            jax.ShapeDtypeStruct(in_grad.shape, in_grad.dtype),
+            jax.ShapeDtypeStruct(new_delta.shape, new_delta.dtype),
+        ),
+        in_specs=[vmem, vmem],
+        out_specs=(vmem, vmem),
+    )(in_grad, new_delta)
 
 
 def solution(mesh):

time: 88 us -> 80.6 us (0.916)
  Pallas kernels: 84 us -> 79.9 us
  local copies, waits for them, and re-layouts: 3.03 us -> 0 us
    pallas_call x1, Pallas kernels: 84 us -> 78.2 us  [on_device(): pl.pallas_call(functools.partial(kernel, nexp, ndp), out_shape=(jax.Shape...]
    unnamed x2 -> x0, local copies, waits for them, and re-layouts: 3.03 us -> none
    pallas_call x0 -> x1, Pallas kernels: none -> 1.69 us  [on_device(): pl.pallas_call(hand_on, out_shape=(jax.ShapeDtypeStruct(in_grad.shape, in...]
where the time goes in v2:
time: 80.6 us; the launch traced here: 80.5 us
  Pallas kernels  79.9 us (99%)
    pallas_call x1, Pallas kernels, on_device(): pl.pallas_call(functools.partial(kernel, nexp, ndp), out_shape=(jax.Shape...  78.2 us
    pallas_call x1, Pallas kernels, on_device(): pl.pallas_call(hand_on, out_shape=(jax.ShapeDtypeStruct(in_grad.shape, in...  1.69 us

profile of v2, /device:TPU:8, one launch (start us, length us, event | category | flops | bytes accessed | tf_op | source)
XLA Modules:
  0.0 80.5 jit_solution(7781587496368164578)
XLA Ops:
  0.6 78.2 %shard_map.122 = (bf16[16,896]{1,0:T(8,128)(2,1)}, f32[1,2,2,128,128]{4,3,2,1,0:T(8,128)}) custom-call(s32[8,16]{1,0:T(8,128)} %bitcast.2, f32[8,16]{1,0:T(8,128)} %bitcast.3, s32[1,2,2]{2,1,0:T(2,128)} %bids.1, bf16[16,7168]{1,0:T(8,128)(2,1)} %tok_hbm.1, bf16[16,7168]{1,0:T(8,128)(2,1)} %og_hbm.1, bf16[1,7168,256]{2,1,0:T(8,128)(2,1)} %wg_hbm.1, ...), custom_call_target="tpu_custom_call" | custom-call | tf_op jit(solution)/shard_map/pallas_call | solution.py:643
  78.8 1.7 %shard_map.123 = (bf16[16,896]{1,0:T(8,128)(2,1)}, f32[1,2,2,128,128]{4,3,2,1,0:T(8,128)}) custom-call(bf16[16,896]{1,0:T(8,128)(2,1)} %get-tuple-element.4.grad_in, f32[1,2,2,128,128]{4,3,2,1,0:T(8,128)} %get-tuple-element.5.delta_in), custom_call_target="tpu_custom_call" | custom-call | tf_op jit(solution)/shard_map/pallas_call | solution.py:668

commit v3 on v2

--- a/solution.py
+++ b/solution.py
@@ -26,15 +26,15 @@
     return tuple((sum(widths[:i]), w) for i, w in enumerate(widths))
 
 
-CHUNKS = cut(128, 256, 256, 256)
+CHUNKS = cut(256, 256, 384)
 NCH = len(CHUNKS)
-GROUPS = cut(128, 256, 256, 256)
+GROUPS = cut(256, 256, 384)
 SUMS = cut(256, 256, 256, 128)
 NSM = len(SUMS)
 BACK = cut(256, 256, 256, 128)
 NBK = len(BACK)
 WIDE = 128
-TAKE_KEYS = (0, 0.6, 0.65, 1.1, 1.15, 1.6, 1.65, 2.1)
+TAKE_KEYS = (0, 0.55, 0.7, 1.05, 1.2, 1.6, 1.75, 2.1)
 GIVE_KEYS = (0, 0.5, 1.6, 2.7)
 
 beta_one = 0.9
@@ -95,8 +95,8 @@
 def kernel(
     nexp,
     ndp,
-    ids_ref,
-    gates_ref,
+    ids_hbm,
+    gates_hbm,
     bids,
     tok_hbm,
     og_hbm,
@@ -108,6 +108,8 @@
     m2_hbm,
     in_grad,
     new_delta,
+    ids_v,
+    gates_v,
     tok_v,
     og_v,
     msg,
@@ -183,23 +185,32 @@
         pltpu.make_async_copy(m1_hbm.at[0], m1_v, load_sem.at[6]),
         pltpu.make_async_copy(m2_hbm.at[0], m2_v, load_sem.at[7]),
     ]
-    for load in loads:
+    tables = [
+        pltpu.make_async_copy(ids_hbm, ids_v, load_sem.at[8]),
+        pltpu.make_async_copy(gates_hbm, gates_v, load_sem.at[9]),
+    ]
+    for load in tables + loads:
         load.start()
 
-    ids_t = ids_ref[...]
-    gates_t = gates_ref[...]
+    for load in tables:
+        load.wait()
+    ids_t = ids_v[...]
+    gates_t = gates_v[...]
     chosen, gates = slot_matrix(ids_t, gates_t, nexp * PAD, 3)
     gate_of = jnp.sum(chosen * gates, axis=1, keepdims=True)
     chosen_b = chosen.astype(BF16)
     loads[0].wait()
     loads[1].wait()
-    for off, width in CHUNKS:
+    def build(c):
+        off, width = CHUNKS[c]
         cols = pl.ds(off, width)
         rows_out = mm(chosen_b, tok_v[:, cols])
         grads_out = mm(chosen_b, og_v[:, cols]) * gate_of
         msg[:, :, cols] = jnp.concatenate(
             [rows_out.reshape(nexp, PAD, width), grads_out.reshape(nexp, PAD, width)], axis=1
         ).astype(BF16)
+
+    build(0)
 
     pl.semaphore_wait(barrier, nexp - 1 + 3)
 
@@ -219,6 +230,8 @@
             ).start()
             return carry
 
+        if c > 0:
+            build(c)
         lax.fori_loop(1, nexp, send, 0)
         own = pltpu.make_async_copy(msg.at[me_e, :, cols], recv.at[me_e, :, cols], a_loc.at[c])
         own.start()
@@ -553,6 +566,12 @@
                 jnp.sqrt(mom_two / corr_two) + adam_eps
             )
 
+    for copy in sent:
+        copy.wait_send()
+    for c, (off, width) in enumerate(CHUNKS):
+        rest = msg.at[pl.ds(0, nexp - 1), :, pl.ds(off, width)]
+        pltpu.make_async_copy(rest, rest, a_send.at[c]).wait()
+
     for c, (off, width) in enumerate(BACK):
         d_own[c].wait()
         rest = recv_d.at[c, pl.ds(0, nexp - 1)]
@@ -562,11 +581,6 @@
         if width > WIDE:
             in_grad[:, pl.ds(off + WIDE, WIDE)] = mm(lower, got).astype(BF16)
 
-    for copy in sent:
-        copy.wait_send()
-    for c, (off, width) in enumerate(CHUNKS):
-        rest = msg.at[pl.ds(0, nexp - 1), :, pl.ds(off, width)]
-        pltpu.make_async_copy(rest, rest, a_send.at[c]).wait()
     for c in range(NBK):
         rest = msg_d.at[c, pl.ds(0, nexp - 1)]
         pltpu.make_async_copy(rest, rest, d_send.at[c]).wait()
@@ -597,6 +611,8 @@
     anym = pl.BlockSpec(memory_space=pl.ANY)
     dma = pltpu.SemaphoreType.DMA
     scratch = [
+        pltpu.VMEM((TOP, TOK), jnp.int32),
+        pltpu.VMEM((TOP, TOK), F32),
         pltpu.VMEM((TOK, FEAT), BF16),
         pltpu.VMEM((TOK, FEAT), BF16),
         pltpu.VMEM((nexp, 16, FEAT), BF16),
@@ -626,7 +642,7 @@
         pltpu.VMEM((ROWS, FEAT), BF16),
         pltpu.VMEM((NBK, nexp, 16, WIDE), BF16),
         pltpu.VMEM((NBK, nexp, 16, WIDE), BF16),
-        dma((8,)),
+        dma((10,)),
         dma((NCH,)),
         dma((NCH,)),
         dma((NCH,)),
@@ -646,7 +662,7 @@
             jax.ShapeDtypeStruct((TOK, FEAT), BF16),
             jax.ShapeDtypeStruct((1, 2, 2, BLK, BLK), F32),
         ),
-        in_specs=[vmem, vmem, smem] + [anym] * 8,
+        in_specs=[anym, anym, smem] + [anym] * 8,
         out_specs=(vmem, vmem),
         scratch_shapes=scratch,
         compiler_params=pltpu.CompilerParams(

time: 80.6 us -> 79.5 us (0.986)
  Pallas kernels: 79.9 us -> 78.7 us
    pallas_call x1, Pallas kernels: 78.2 us -> 77 us  [on_device(): pl.pallas_call(functools.partial(kernel, nexp, ndp), out_shape=(jax.Shape...]
where the time goes in v3:
time: 79.5 us; the launch traced here: 79.4 us
  Pallas kernels  78.7 us (99%)
    pallas_call x1, Pallas kernels, on_device(): pl.pallas_call(functools.partial(kernel, nexp, ndp), out_shape=(jax.Shape...  77 us
    pallas_call x1, Pallas kernels, on_device(): pl.pallas_call(hand_on, out_shape=(jax.ShapeDtypeStruct(in_grad.shape, in...  1.69 us

profile of v3, /device:TPU:8, one launch (start us, length us, event | category | flops | bytes accessed | tf_op | source)
XLA Modules:
  0.0 79.4 jit_solution(1890662288928657241)
XLA Ops:
  0.6 77.0 %shard_map.122 = (bf16[16,896]{1,0:T(8,128)(2,1)}, f32[1,2,2,128,128]{4,3,2,1,0:T(8,128)}) custom-call(s32[8,16]{1,0:T(8,128)} %bitcast.2, f32[8,16]{1,0:T(8,128)} %bitcast.3, s32[1,2,2]{2,1,0:T(2,128)} %bids.1, bf16[16,7168]{1,0:T(8,128)(2,1)} %tok_hbm.1, bf16[16,7168]{1,0:T(8,128)(2,1)} %og_hbm.1, bf16[1,7168,256]{2,1,0:T(8,128)(2,1)} %wg_hbm.1, ...), custom_call_target="tpu_custom_call" | custom-call | tf_op jit(solution)/shard_map/pallas_call | solution.py:659
  77.7 1.7 %shard_map.123 = (bf16[16,896]{1,0:T(8,128)(2,1)}, f32[1,2,2,128,128]{4,3,2,1,0:T(8,128)}) custom-call(bf16[16,896]{1,0:T(8,128)(2,1)} %get-tuple-element.4.grad_in, f32[1,2,2,128,128]{4,3,2,1,0:T(8,128)} %get-tuple-element.5.delta_in), custom_call_target="tpu_custom_call" | custom-call | tf_op jit(solution)/shard_map/pallas_call | solution.py:684

commit v4 on v3

--- a/solution.py
+++ b/solution.py
@@ -29,11 +29,11 @@
 CHUNKS = cut(256, 256, 384)
 NCH = len(CHUNKS)
 GROUPS = cut(256, 256, 384)
-SUMS = cut(256, 256, 256, 128)
+SUMS = cut(384, 256, 256)
 NSM = len(SUMS)
-BACK = cut(256, 256, 256, 128)
+BACK = cut(384, 256, 256)
 NBK = len(BACK)
-WIDE = 128
+WIDE = tuple(128 if width <= 256 else 256 for _, width in BACK)
 TAKE_KEYS = (0, 0.55, 0.7, 1.05, 1.2, 1.6, 1.75, 2.1)
 GIVE_KEYS = (0, 0.5, 1.6, 2.7)
 
@@ -509,14 +509,18 @@
                     copy.wait_recv()
         total = own_t[:, cols] + from_l[:, cols].astype(F32) + from_r[:, cols].astype(F32)
         wide = mm(spread, total.astype(BF16)).reshape(nexp, PAD, width)
-        second = wide[:, :, WIDE:] if width > WIDE else jnp.zeros((nexp, PAD, WIDE), F32)
-        msg_d[c] = jnp.concatenate([wide[:, :, :WIDE], second], axis=1).astype(BF16)
+        half = WIDE[c]
+        second = wide[:, :, half:]
+        if width < 2 * half:
+            blank = jnp.zeros((nexp, PAD, 2 * half - width), F32)
+            second = blank if width == half else jnp.concatenate([second, blank], axis=2)
+        msg_d[c, :, :, :half] = jnp.concatenate([wide[:, :, :half], second], axis=1).astype(BF16)
 
         def send(i, carry):
             to = lax.rem(me_e + i, nexp)
             pltpu.make_async_remote_copy(
-                src_ref=msg_d.at[c, to],
-                dst_ref=recv_d.at[c, me_e],
+                src_ref=msg_d.at[c, to, :, pl.ds(0, WIDE[c])],
+                dst_ref=recv_d.at[c, me_e, :, pl.ds(0, WIDE[c])],
                 send_sem=d_send.at[c],
                 recv_sem=d_recv.at[c],
                 device_id={"expert": to},
@@ -525,7 +529,10 @@
             return carry
 
         lax.fori_loop(1, nexp, send, 0)
-        own = pltpu.make_async_copy(msg_d.at[c, me_e], recv_d.at[c, me_e], d_loc.at[c])
+        cells = pl.ds(0, WIDE[c])
+        own = pltpu.make_async_copy(
+            msg_d.at[c, me_e, :, cells], recv_d.at[c, me_e, :, cells], d_loc.at[c]
+        )
         own.start()
         d_own.append(own)
 
@@ -574,15 +581,17 @@
 
     for c, (off, width) in enumerate(BACK):
         d_own[c].wait()
-        rest = recv_d.at[c, pl.ds(0, nexp - 1)]
+        half = WIDE[c]
+        rest = recv_d.at[c, pl.ds(0, nexp - 1), :, pl.ds(0, half)]
         pltpu.make_async_copy(rest, rest, d_recv.at[c]).wait()
-        got = recv_d[c].reshape(nexp * 16, WIDE)
-        in_grad[:, pl.ds(off, WIDE)] = mm(upper, got).astype(BF16)
-        if width > WIDE:
-            in_grad[:, pl.ds(off + WIDE, WIDE)] = mm(lower, got).astype(BF16)
+        got = recv_d[c, :, :, :half].reshape(nexp * 16, half)
+        in_grad[:, pl.ds(off, half)] = mm(upper, got).astype(BF16)
+        tail = width - half
+        if tail > 0:
+            in_grad[:, pl.ds(off + half, tail)] = mm(lower, got[:, :tail]).astype(BF16)
 
     for c in range(NBK):
-        rest = msg_d.at[c, pl.ds(0, nexp - 1)]
+        rest = msg_d.at[c, pl.ds(0, nexp - 1), :, pl.ds(0, WIDE[c])]
         pltpu.make_async_copy(rest, rest, d_send.at[c]).wait()
 
 
@@ -640,8 +649,8 @@
         pltpu.VMEM((HALF, FEAT), BF16),
         pltpu.VMEM((ROWS, FEAT), BF16),
         pltpu.VMEM((ROWS, FEAT), BF16),
-        pltpu.VMEM((NBK, nexp, 16, WIDE), BF16),
-        pltpu.VMEM((NBK, nexp, 16, WIDE), BF16),
+        pltpu.VMEM((NBK, nexp, 16, max(WIDE)), BF16),
+        pltpu.VMEM((NBK, nexp, 16, max(WIDE)), BF16),
         dma((10,)),
         dma((NCH,)),
         dma((NCH,)),

time: 79.5 us -> 79.4 us (level)
  no operation moved by 1% of the time
where the time goes in v4:
time: 79.4 us; the launch traced here: 79.3 us
  Pallas kernels  78.6 us (99%)
    pallas_call x1, Pallas kernels, on_device(): pl.pallas_call(functools.partial(kernel, nexp, ndp), out_shape=(jax.Shape...  76.9 us
    pallas_call x1, Pallas kernels, on_device(): pl.pallas_call(hand_on, out_shape=(jax.ShapeDtypeStruct(in_grad.shape, in...  1.69 us

profile of v4, /device:TPU:8, one launch (start us, length us, event | category | flops | bytes accessed | tf_op | source)
XLA Modules:
  0.0 79.3 jit_solution(7304456650167009880)
XLA Ops:
  0.6 76.9 %shard_map.122 = (bf16[16,896]{1,0:T(8,128)(2,1)}, f32[1,2,2,128,128]{4,3,2,1,0:T(8,128)}) custom-call(s32[8,16]{1,0:T(8,128)} %bitcast.2, f32[8,16]{1,0:T(8,128)} %bitcast.3, s32[1,2,2]{2,1,0:T(2,128)} %bids.1, bf16[16,7168]{1,0:T(8,128)(2,1)} %tok_hbm.1, bf16[16,7168]{1,0:T(8,128)(2,1)} %og_hbm.1, bf16[1,7168,256]{2,1,0:T(8,128)(2,1)} %wg_hbm.1, ...), custom_call_target="tpu_custom_call" | custom-call | tf_op jit(solution)/shard_map/pallas_call | solution.py:668
  77.6 1.7 %shard_map.123 = (bf16[16,896]{1,0:T(8,128)(2,1)}, f32[1,2,2,128,128]{4,3,2,1,0:T(8,128)}) custom-call(bf16[16,896]{1,0:T(8,128)(2,1)} %get-tuple-element.4.grad_in, f32[1,2,2,128,128]{4,3,2,1,0:T(8,128)} %get-tuple-element.5.delta_in), custom_call_target="tpu_custom_call" | custom-call | tf_op jit(solution)/shard_map/pallas_call | solution.py:693
